TPU v7x, 32 devices: a whole 2x2x4 slice. The times are simulated.
32 devices in a mesh: row: 8 (over z, core), col: 4 (over y, x).
Axes of the slice: x: 2, y: 2, z: 4, core: 2. Of those that a mesh axis runs over, the one named last changes fastest.
Arguments:
- blocks: bfloat16 [8, 4, 5, 128, 8192], P('row', 'col'), may hold values from -6 to 6
- coords: int32 [8, 4, 5, 3], P('row', 'col'), may hold values from 0 to 7, as said below
- counts: int32 [8, 4], P('row', 'col'), may hold values from 1 to 5, as said below
- doc_factor: bfloat16 [4096, 128], P(('col', 'row')), may hold values from -6 to 6
- ctx_factor: bfloat16 [512, 128], P('col'), may hold values from -0.0625 to 0.0625
Outputs:
- mttkrp: float32 [4096, 128], P(('row', 'col'))
Inputs may be any that keep to these rules, and one draw needn't show every extreme that they name: coords[..., 0] lies in 0 to 3, coords[..., 1] in 0 to 7, coords[..., 2] in 0 to 7; slots at or past the device's count are ignored. `counts`: some device uses all 5 slots.
All inputs are finite; a program needn't handle non-finite values.
Results may differ from a plain program's by a relative error of at most 0.0029.
Values may be sent and summed in bfloat16 or wider, within the bound.
A program may use at most 64 MiB of HBM per device.

v0:
```python
import jax
import jax.numpy as jnp
from jax import lax
from jax.sharding import PartitionSpec as P

BQ = 128
BD = 128
BK = 64
QBC = 1


def kr_table(brows, crows):
    table = brows[:, None, :].astype(jnp.float32) * crows[None, :, :].astype(jnp.float32)
    return table.reshape(brows.shape[0] * crows.shape[0], brows.shape[1]).astype(jnp.bfloat16)


def body(blocks, coords, counts, doc_factor, ctx_factor):
    doc_slab = lax.all_gather(doc_factor, "row", axis=0, tiled=True)
    ctx_all = lax.all_gather(ctx_factor, "col", axis=0, tiled=True)
    own_blocks = blocks[0, 0]
    own_coords = coords[0, 0]
    used = counts[0, 0]
    rank = doc_slab.shape[1]
    dev_rows = QBC * BQ
    all_rows = dev_rows * lax.axis_size("col")
    start = jnp.int32(0)
    empty = jnp.zeros((all_rows, rank), jnp.float32)

    def step(index, acc):
        place = own_coords[index]
        qstart = place[0] * BQ
        inside = jnp.logical_and(qstart >= start, qstart < start + all_rows)

        def add_term(inner):
            brows = lax.dynamic_slice_in_dim(doc_slab, place[1] * BD, BD, 0)
            crows = lax.dynamic_slice_in_dim(ctx_all, place[2] * BK, BK, 0)
            term = jnp.dot(
                own_blocks[index], kr_table(brows, crows), preferred_element_type=jnp.float32
            )
            local = jnp.clip(qstart, 0, all_rows - BQ)
            current = lax.dynamic_slice_in_dim(inner, local, BQ, 0)
            return lax.dynamic_update_slice_in_dim(inner, current + term, local, 0)

        return lax.cond(inside, add_term, lambda inner: inner, acc)

    partial_value = lax.fori_loop(0, used, step, empty)
    return lax.psum_scatter(partial_value, "col", scatter_dimension=0, tiled=True)


def solution(mesh):
    placed = (
        P("row", "col", None, None, None),
        P("row", "col", None, None),
        P("row", "col"),
        P(("col", "row"), None),
        P("col", None),
    )
    return jax.shard_map(
        body, mesh=mesh, in_specs=placed, out_specs=P(("row", "col"), None), check_vma=False
    )
```

profile of v0, /device:TPU:0, one launch (start us, length us, event | category | flops | bytes accessed | tf_op | source)
XLA Modules:
  0.0 94.6 jit_solution(18133102123350628783)
XLA Ops:
  6.5 0.0 reduce-scatter.2.cloned.1.call-start
  6.5 16.1 %all_gather.6 = bf16[1024,128]{1,0:T(8,128)(2,1)S(1)} all-gather(bf16[128,128]{1,0:T(8,128)(2,1)} %param.12), channel_id=1, replica_groups=mesh['row'=8,'col'=4] {'row'}, dimensions={0}, use_global_device_ids=true | all-gather | bytes 294912 | tf_op jit(solution)/shard_map/all_gather | solution.py:18
  22.6 8.7 %all_gather.7 = bf16[512,128]{1,0:T(8,128)(2,1)S(1)} all-gather(bf16[128,128]{1,0:T(8,128)(2,1)} %param.13), channel_id=1, replica_groups=mesh['row'=8,'col'=4] {'col'}, dimensions={0}, use_global_device_ids=true | all-gather | bytes 163840 | tf_op jit(solution)/shard_map/all_gather | solution.py:19
  31.3 0.8 copy.7
  32.1 6.9 %while.13 = (s32[]{:T(128)}, f32[512,128]{1,0:T(8,128)S(1)}, s32[]{:T(128)}, s32[5,3]{1,0:T(8,128)S(1)}, bf16[5,128,8192]{2,1,0:T(8,128)(2,1)}, /*index=5*/bf16[...) while((s32[]{:T(128)}, f32[512,128]{1,0:T(8,128)S(1)}, ...), condition=%wide.region_3.4_spmd, body=%wide.region_0.3_spmd.sunk | while | flops 270573568 | bytes 6799827 | solution.py:46
  32.8 5.5 %conditional.2 = (f32[512,128]{1,0:T(8,128)S(1)}) conditional(s32[]{:T(128)} %convert_element_type.27, f32[512,128]{1,0:T(8,128)S(1)} %get-tuple-element.150, (s32[]{:T(128)}, f32[512,128]{1,0:T(8,128)S(1)}, s32[]{:T(128)}, bf16[5,128,8192]{2,1,0:T(8,128)(2,1)}, s32[1,3]{1,0:T(1,128)S(1)}, /*index=5*/bf16[1024,128]{1,0:T(8,128)(2,1)S(1)}, ...), branch_computations={%region_1.0_spmd, %region_2.2_spmd} | conditional | flops 270573568 | bytes 6799554 | solution.py:44
  32.8 0.7 fusion.7
  34.8 0.6 multiply_convert_fusion
  35.4 2.3 %fusion.3 = f32[128,128]{1,0:T(8,128)S(1)} fusion(bf16[8192,128]{1,0:T(8,128)(2,1)S(1)} %bitcast.18, bf16[5,128,8192]{2,1,0:T(8,128)(2,1)} %get-tuple-element.54, s32[]{:T(128)S(6)} %select_n.2, f32[512,128]{1,0:T(8,128)S(1)} %get-tuple-element.52, s32[]{:T(128)S(6)} %min.3), kind=kOutput, calls=%fused_computation.4 | convolution fusion | flops 268451840 | bytes 4325384 | tf_op jit(solution)/shard_map/while/body/cond/branch_1_fun/dot_general | solution.py:37
  37.7 0.6 dynamic_update_slice.2
  38.9 0.0 copy-start
  38.9 0.7 copy-done
  39.6 0.0 reduce-scatter.2.cloned.1.call-update
  39.7 48.0 %reduce-scatter.2.cloned.1.call-done = f32[128,128]{1,0:T(8,128)} async-done(((f32[512,128]{1,0:T(8,128)}), f32[128,128]{1,0:T(8,128)}) %reduce-scatter.2.cloned.1.call-update) | async-done | bytes 65552 | tf_op jit(solution)/shard_map/reduce_scatter | solution.py:47
  (4 shorter events, 0.1 us)
Async XLA Ops:
  6.5 81.2 %reduce-scatter.2.cloned.1.call-start = ((), (), s32[]{:S(2)}) async-start(), calls=%async_computation.1 | async-start | bytes 327680 | tf_op jit(solution)/shard_map/reduce_scatter | solution.py:47
  38.9 0.7 copy-start
Sparse Core Ops, SparseCore 0:
  39.8 47.8 reduce-scatter.1
where the time goes:
time: 94.6 us
  waiting for transfers between devices  48.1 us (51%)
  blocking collectives  24.7 us (26%)
  between operations  13.4 us (14%)
  local copies, waits for them, and re-layouts  2.7 us (3%)
  loops' own time  2.7 us (3%)
  matrix products  2.29 us (2%)
    reduce_scatter x1, waiting for transfers between devices, body(): lax.psum_scatter(partial_value, 'col', scatter_dimension=0, tiled=True)  48 us
    all_gather x1, blocking collectives, body(): doc_slab = lax.all_gather(doc_factor, 'row', axis=0, tiled=True)  16.1 us
    all_gather x1, blocking collectives, body(): ctx_all = lax.all_gather(ctx_factor, 'col', axis=0, tiled=True)  8.66 us
    dot_general x1, matrix products, add_term(): jnp.dot(own_blocks[index], kr_table(brows, crows), preferred_element_type...  2.29 us
  transfers between devices with their start and end apart: 1, of which 1 were waited for; matrix products, arithmetic and copies ran while one was open for 0% of the time, Pallas kernels for 0%

commit v1 on v0

v1 whole, which is shorter than its diff:
```python
import functools

import jax
import jax.numpy as jnp
from jax import lax
from jax.experimental import pallas as pl
from jax.experimental.pallas import tpu as pltpu
from jax.sharding import PartitionSpec as P

BQ = 128
BD = 128
BK = 64
CHUNKS = 4
SEND = jnp.bfloat16
MESH = pl.DeviceIdType.MESH


def kernel(
    nrow, ncol, blocks, coords_hbm, counts_hbm, doc, ctx, out,
    coords, counts, xbuf, ctx_all, term, outbox, inbox,
    x_sem, own_sem, doc_send, doc_recv, sib_send, sib_recv, ctx_sem,
    ctx_send, ctx_recv, sum_send, sum_recv, *slabs,
):
    slots = xbuf.shape[0]
    nz = nrow // 2
    rows = BD // CHUNKS
    depth = rows * BK
    unit = ctx_all.shape[1]
    units = ctx.shape[0] // unit
    per_block = BK // unit
    me_r, me_c = lax.axis_index("row"), lax.axis_index("col")
    z, core = lax.div(me_r, 2), lax.rem(me_r, 2)
    sibling = z * 2 + (1 - core)

    def chip(j):
        return lax.rem(z + j + nz, nz) * 2 + core

    def column(j):
        return lax.rem(me_c + j + ncol, ncol)

    def load(h, s):
        return pltpu.make_async_copy(
            blocks.at[0, 0, s, :, pl.ds(h * depth, depth)],
            xbuf.at[s, :, pl.ds(h * depth, depth)],
            x_sem.at[h, s],
        )

    own_docs = [
        pltpu.make_async_copy(doc.at[pl.ds(h * rows, rows)], slabs[h].at[me_r], own_sem.at[2 + h])
        for h in range(CHUNKS)
    ]
    own_ctx = [
        pltpu.make_async_copy(
            ctx.at[pl.ds(i * unit, unit)], ctx_all.at[me_c * units + i], ctx_sem.at[i]
        )
        for i in range(units)
    ]
    own_coords = pltpu.make_async_copy(coords_hbm, coords, own_sem.at[0])
    own_counts = pltpu.make_async_copy(counts_hbm, counts, own_sem.at[1])
    own_coords.start()
    own_counts.start()
    for copy in own_docs + own_ctx:
        copy.start()
    for h in range(CHUNKS):
        for s in range(slots):
            load(h, s).start()

    barrier = pltpu.get_barrier_semaphore()
    peers = [(chip(j), me_c) for j in range(1, nz)] + [(sibling, me_c)]
    peers += [(me_r, column(j)) for j in range(1, ncol)]
    for peer in peers:
        pl.semaphore_signal(barrier, inc=1, device_id=peer, device_id_type=MESH)
    pl.semaphore_wait(barrier, len(peers))

    def send_ctx(j, i):
        return pltpu.make_async_remote_copy(
            src_ref=ctx.at[pl.ds(i * unit, unit)],
            dst_ref=ctx_all.at[me_c * units + i],
            send_sem=ctx_send.at[j, i], recv_sem=ctx_recv.at[j, i],
            device_id=(me_r, column(j)), device_id_type=MESH,
        )

    def slab_rows(row, h):
        return slabs[h].at[row]

    def send_doc(h, j):
        return pltpu.make_async_remote_copy(
            src_ref=doc.at[pl.ds(h * rows, rows)],
            dst_ref=slab_rows(me_r, h),
            send_sem=doc_send.at[h, j], recv_sem=doc_recv.at[h, j],
            device_id=(chip(j), me_c), device_id_type=MESH,
        )

    def send_sibling(h, j):
        return pltpu.make_async_remote_copy(
            src_ref=doc.at[pl.ds(h * rows, rows)] if j == 0 else slab_rows(chip(-j), h),
            dst_ref=slab_rows(me_r if j == 0 else chip(-j), h),
            send_sem=sib_send.at[h, j], recv_sem=sib_recv.at[h, j],
            device_id=(sibling, me_c), device_id_type=MESH,
        )

    for j in range(1, ncol):
        for i in range(units):
            send_ctx(j, i).start()
    for h in range(CHUNKS):
        for j in range(1, nz):
            send_doc(h, j).start()
        send_sibling(h, 0).start()

    def relay(h):
        for j in range(1, nz):
            send_doc(h, j).wait_recv()
            send_sibling(h, j).start()

    relay(0)
    own_coords.wait()
    own_counts.wait()
    for copy in own_docs + own_ctx:
        copy.wait()
    for j in range(1, ncol):
        for i in range(units):
            send_ctx(j, i).wait_recv()

    def multiply(h, s):
        load(h, s).wait()
        brows = slabs[h][coords[0, 1, 0, s]].astype(jnp.float32)
        first = coords[0, 2, 0, s] * per_block
        crows = jnp.concatenate([ctx_all[first + i] for i in range(per_block)], axis=0)
        crows = crows.reshape(BK // 16, 16, crows.shape[1])
        parts = []
        for b in range(rows):
            brow = jnp.broadcast_to(brows[b:b + 1, :], (16, brows.shape[1])).astype(jnp.bfloat16)
            parts.append((crows * brow[None]).reshape(BK, brows.shape[1]))
        table = jnp.concatenate(parts, axis=0)
        got = jnp.dot(
            xbuf[s, :, h * depth:(h + 1) * depth], table, preferred_element_type=jnp.float32
        )
        if h == 0:
            term[s] = got
        else:
            term[s] += got

    middle = (slots + 1) // 2
    for h in range(CHUNKS):
        for j in range(nz):
            send_sibling(h, j).wait_recv()

        def step(s, carry, h=h):
            multiply(h, s)
            return carry

        lax.fori_loop(0, middle, step, 0)
        if h + 1 < CHUNKS:
            relay(h + 1)
        lax.fori_loop(middle, slots, step, 0)

    used = counts[0, 0]

    def partial_sum(q):
        total = jnp.zeros(out.shape, jnp.float32)
        for s in range(slots):
            wanted = jnp.logical_and(
                jnp.full(out.shape, coords[0, 0, 0, s]) == q, jnp.full(out.shape, used) > s
            )
            total += jnp.where(wanted, term[s], 0.0)
        return total

    def send_sum(j):
        return pltpu.make_async_remote_copy(
            src_ref=outbox.at[j], dst_ref=inbox.at[j],
            send_sem=sum_send.at[j], recv_sem=sum_recv.at[j],
            device_id=(me_r, column(j)), device_id_type=MESH,
        )

    for j in range(1, ncol):
        outbox[j] = partial_sum(column(j)).astype(outbox.dtype)
        send_sum(j).start()
    total = partial_sum(me_c)
    for j in range(1, ncol):
        send_sum(j).wait_recv()
        total += inbox[j].astype(jnp.float32)
    out[...] = total

    for j in range(1, ncol):
        for i in range(units):
            send_ctx(j, i).wait_send()
        send_sum(j).wait_send()
    for h in range(CHUNKS):
        for j in range(1, nz):
            send_doc(h, j).wait_send()
        for j in range(nz):
            send_sibling(h, j).wait_send()


def body(nrow, ncol, blocks, coords, counts, doc_factor, ctx_factor):
    slots, width = blocks.shape[2], blocks.shape[4]
    rank = doc_factor.shape[1]
    nz = nrow // 2
    unit = min(BK, ctx_factor.shape[0])
    units = ctx_factor.shape[0] // unit
    dma = pltpu.SemaphoreType.DMA
    return pl.pallas_call(
        functools.partial(kernel, nrow, ncol),
        out_shape=jax.ShapeDtypeStruct((BQ, rank), jnp.float32),
        in_specs=[
            pl.BlockSpec(memory_space=pltpu.HBM),
            pl.BlockSpec(memory_space=pltpu.HBM),
            pl.BlockSpec(memory_space=pltpu.HBM),
            pl.BlockSpec(memory_space=pltpu.HBM),
            pl.BlockSpec(memory_space=pltpu.HBM),
        ],
        out_specs=pl.BlockSpec(memory_space=pltpu.VMEM),
        scratch_shapes=[
            pltpu.SMEM((1, 3, 1, slots), jnp.int32),
            pltpu.SMEM((1, 1), jnp.int32),
            pltpu.VMEM((slots, BQ, width), jnp.bfloat16),
            pltpu.VMEM((ctx_factor.shape[0] * ncol // unit, unit, rank), jnp.bfloat16),
            pltpu.VMEM((slots, BQ, rank), jnp.float32),
            pltpu.VMEM((ncol, BQ, rank), SEND),
            pltpu.VMEM((ncol, BQ, rank), SEND),
            dma((CHUNKS, slots)),
            dma((2 + CHUNKS,)),
            dma((CHUNKS, nz)),
            dma((CHUNKS, nz)),
            dma((CHUNKS, nz)),
            dma((CHUNKS, nz)),
            dma((units,)),
            dma((ncol, units)),
            dma((ncol, units)),
            dma((ncol,)),
            dma((ncol,)),
        ] + [pltpu.VMEM((nrow, BD // CHUNKS, rank), jnp.bfloat16)] * CHUNKS,
        compiler_params=pltpu.CompilerParams(
            collective_id=0, has_side_effects=True, vmem_limit_bytes=60 * 1024 * 1024
        ),
        cost_estimate=pl.CostEstimate(
            flops=2 * slots * BQ * width * rank,
            bytes_accessed=slots * BQ * width * 2,
            transcendentals=0,
        ),
    )(blocks, coords.transpose(0, 3, 1, 2), counts, doc_factor, ctx_factor)


def solution(mesh):
    placed = (
        P("row", "col", None, None, None),
        P("row", "col", None, None),
        P("row", "col"),
        P(("col", "row"), None),
        P("col", None),
    )
    return jax.shard_map(
        functools.partial(body, mesh.shape["row"], mesh.shape["col"]),
        mesh=mesh, in_specs=placed, out_specs=P(("row", "col"), None), check_vma=False,
    )
```

time: 94.6 us -> 24.3 us (0.26)
  waiting for transfers between devices: 48.1 us -> 0 us
  blocking collectives: 24.7 us -> 0 us
  Pallas kernels: 0 us -> 22.1 us
  between operations: 13.4 us -> 0.66 us
  loops' own time: 2.7 us -> 0 us
  matrix products: 2.29 us -> 0 us
  local copies, waits for them, and re-layouts: 2.7 us -> 1.47 us
    reduce_scatter x1 -> x0, waiting for transfers between devices: 48 us -> none  [body(): lax.psum_scatter(partial_value, 'col', scatter_dimension=0, tiled=True)]
    all_gather x2 -> x0, blocking collectives: 24.7 us -> none  [the longest x1 16.1 us: body(): doc_slab = lax.all_gather(doc_factor, 'row', axis=0, tiled=True)]
    pallas_call x0 -> x1, Pallas kernels: none -> 22.1 us  [body(): pl.pallas_call(functools.partial(kernel, nrow, ncol), out_shape=jax.Shape...]
    another operation x2 -> x0, loops' own time: 2.7 us -> none  [the longest x1 1.38 us: body(): partial_value = lax.fori_loop(0, used, step, empty)]
    dot_general x1 -> x0, matrix products: 2.29 us -> none  [add_term(): jnp.dot(own_blocks[index], kr_table(brows, crows), preferred_element_type...]
  transfers between devices with their start and end apart: 1 -> 0, of which waited for: 1 -> 0; matrix products, arithmetic and copies ran while one was open for 0% -> 0% of each run, Pallas kernels for 0% -> 0%
where the time goes in v1:
time: 24.3 us; the launch traced here: 24.2 us
  Pallas kernels  22.1 us (91%)
  local copies, waits for them, and re-layouts  1.47 us (6%)
  between operations  0.66 us (3%)
    pallas_call x1, Pallas kernels, body(): pl.pallas_call(functools.partial(kernel, nrow, ncol), out_shape=jax.Shape...  22.1 us
    unnamed x1, local copies, waits for them, and re-layouts  1.47 us

profile of v1, /device:TPU:0, one launch (start us, length us, event | category | flops | bytes accessed | tf_op | source)
XLA Modules:
  0.0 24.2 jit_solution(9673743021614364512)
XLA Ops:
  0.7 22.1 %shard_map.55 = f32[128,128]{1,0:T(8,128)} custom-call(bf16[1,1,5,128,8192]{4,3,2,1,0:T(8,128)(2,1)} %blocks.1, s32[1,3,1,5]{3,2,1,0:T(1,128)} %bitcast.1, s32[1,1]{1,0:T(1,128)S(6)} %copy.7.counts_hbm, bf16[128,128]{1,0:T(8,128)(2,1)} %doc.1, bf16[128,128]{1,0:T(8,128)(2,1)} %ctx.1), custom_call_target="tpu_custom_call" | custom-call | flops 1342177280 | bytes 10485760 | tf_op jit(solution)/shard_map/pallas_call | solution.py:202
  22.7 1.5 %copy.8 = f32[128,128]{1,0:T(8,128)} copy(f32[128,128]{1,0:T(8,128)} %shard_map.55) | data formatting | bytes 131072

commit v2 on v1

--- a/solution.py
+++ b/solution.py
@@ -10,7 +10,7 @@
 BQ = 128
 BD = 128
 BK = 64
-CHUNKS = 4
+CHUNKS = 2
 SEND = jnp.bfloat16
 MESH = pl.DeviceIdType.MESH
 
@@ -45,6 +45,12 @@
             x_sem.at[h, s],
         )
 
+    barrier = pltpu.get_barrier_semaphore()
+    peers = [(chip(j), me_c) for j in range(1, nz)] + [(sibling, me_c)]
+    peers += [(me_r, column(j)) for j in range(1, ncol)]
+    for peer in peers:
+        pl.semaphore_signal(barrier, inc=1, device_id=peer, device_id_type=MESH)
+
     own_docs = [
         pltpu.make_async_copy(doc.at[pl.ds(h * rows, rows)], slabs[h].at[me_r], own_sem.at[2 + h])
         for h in range(CHUNKS)
@@ -65,11 +71,6 @@
         for s in range(slots):
             load(h, s).start()
 
-    barrier = pltpu.get_barrier_semaphore()
-    peers = [(chip(j), me_c) for j in range(1, nz)] + [(sibling, me_c)]
-    peers += [(me_r, column(j)) for j in range(1, ncol)]
-    for peer in peers:
-        pl.semaphore_signal(barrier, inc=1, device_id=peer, device_id_type=MESH)
     pl.semaphore_wait(barrier, len(peers))
 
     def send_ctx(j, i):
@@ -149,10 +150,12 @@
             multiply(h, s)
             return carry
 
-        lax.fori_loop(0, middle, step, 0)
         if h + 1 < CHUNKS:
+            lax.fori_loop(0, middle, step, 0)
             relay(h + 1)
-        lax.fori_loop(middle, slots, step, 0)
+            lax.fori_loop(middle, slots, step, 0)
+        else:
+            lax.fori_loop(0, slots, step, 0)
 
     used = counts[0, 0]
 

time: 24.3 us -> 21.8 us (0.90)
  Pallas kernels: 22.1 us -> 19.5 us
    pallas_call x1, Pallas kernels: 22.1 us -> 19.5 us  [body(): pl.pallas_call(functools.partial(kernel, nrow, ncol), out_shape=jax.Shape...]
where the time goes in v2:
time: 21.8 us; the launch traced here: 21.7 us
  Pallas kernels  19.5 us (89%)
  local copies, waits for them, and re-layouts  1.47 us (7%)
  between operations  0.66 us (3%)
    pallas_call x1, Pallas kernels, body(): pl.pallas_call(functools.partial(kernel, nrow, ncol), out_shape=jax.Shape...  19.5 us
    unnamed x1, local copies, waits for them, and re-layouts  1.47 us

profile of v2, /device:TPU:0, one launch (start us, length us, event | category | flops | bytes accessed | tf_op | source)
XLA Modules:
  0.0 21.7 jit_solution(3499125644614824864)
XLA Ops:
  0.7 19.5 %shard_map.55 = f32[128,128]{1,0:T(8,128)} custom-call(bf16[1,1,5,128,8192]{4,3,2,1,0:T(8,128)(2,1)} %blocks.1, s32[1,3,1,5]{3,2,1,0:T(1,128)} %bitcast.1, s32[1,1]{1,0:T(1,128)S(6)} %copy.7.counts_hbm, bf16[128,128]{1,0:T(8,128)(2,1)} %doc.1, bf16[128,128]{1,0:T(8,128)(2,1)} %ctx.1), custom_call_target="tpu_custom_call" | custom-call | flops 1342177280 | bytes 10485760 | tf_op jit(solution)/shard_map/pallas_call | solution.py:205
  20.2 1.5 %copy.8 = f32[128,128]{1,0:T(8,128)} copy(f32[128,128]{1,0:T(8,128)} %shard_map.55) | data formatting | bytes 131072

commit v3 on v2

--- a/solution.py
+++ b/solution.py
@@ -132,10 +132,20 @@
         for b in range(rows):
             brow = jnp.broadcast_to(brows[b:b + 1, :], (16, brows.shape[1])).astype(jnp.bfloat16)
             parts.append((crows * brow[None]).reshape(BK, brows.shape[1]))
-        table = jnp.concatenate(parts, axis=0)
-        got = jnp.dot(
-            xbuf[s, :, h * depth:(h + 1) * depth], table, preferred_element_type=jnp.float32
-        )
+        half = depth // 2
+        table = jnp.concatenate(
+            [jnp.concatenate(parts[:rows // 2], axis=0), jnp.concatenate(parts[rows // 2:], axis=0)],
+            axis=1,
+        )
+        left = jnp.concatenate(
+            [
+                xbuf[s, :, h * depth:h * depth + half],
+                xbuf[s, :, h * depth + half:(h + 1) * depth],
+            ],
+            axis=0,
+        )
+        both = jnp.dot(left, table, preferred_element_type=jnp.float32)
+        got = both[:BQ, :brows.shape[1]] + both[BQ:, brows.shape[1]:]
         if h == 0:
             term[s] = got
         else:

time: 21.8 us -> 22 us (level)
  no operation moved by 1% of the time
where the time goes in v3:
time: 22 us; the launch traced here: 21.8 us
  Pallas kernels  19.7 us (90%)
  local copies, waits for them, and re-layouts  1.47 us (7%)
  between operations  0.66 us (3%)
    pallas_call x1, Pallas kernels, body(): pl.pallas_call(functools.partial(kernel, nrow, ncol), out_shape=jax.Shape...  19.7 us
    unnamed x1, local copies, waits for them, and re-layouts  1.47 us

profile of v3, /device:TPU:0, one launch (start us, length us, event | category | flops | bytes accessed | tf_op | source)
XLA Modules:
  0.0 21.8 jit_solution(14696276764985853791)
XLA Ops:
  0.7 19.7 %shard_map.55 = f32[128,128]{1,0:T(8,128)} custom-call(bf16[1,1,5,128,8192]{4,3,2,1,0:T(8,128)(2,1)} %blocks.1, s32[1,3,1,5]{3,2,1,0:T(1,128)} %bitcast.1, s32[1,1]{1,0:T(1,128)S(6)} %copy.7.counts_hbm, bf16[128,128]{1,0:T(8,128)(2,1)} %doc.1, bf16[128,128]{1,0:T(8,128)(2,1)} %ctx.1), custom_call_target="tpu_custom_call" | custom-call | flops 1342177280 | bytes 10485760 | tf_op jit(solution)/shard_map/pallas_call | solution.py:215
  20.4 1.5 %copy.8 = f32[128,128]{1,0:T(8,128)} copy(f32[128,128]{1,0:T(8,128)} %shard_map.55) | data formatting | bytes 131072

commit v4 on v2

--- a/solution.py
+++ b/solution.py
@@ -11,13 +11,14 @@
 BD = 128
 BK = 64
 CHUNKS = 2
+PIECE = 8
 SEND = jnp.bfloat16
 MESH = pl.DeviceIdType.MESH
 
 
 def kernel(
-    nrow, ncol, blocks, coords_hbm, counts_hbm, doc, ctx, out,
-    coords, counts, xbuf, ctx_all, term, outbox, inbox,
+    nrow, ncol, blocks, coords_hbm, counts_hbm, doc, ctx, out, inbox,
+    coords, counts, xbuf, ctx_all, term, outbox, own,
     x_sem, own_sem, doc_send, doc_recv, sib_send, sib_recv, ctx_sem,
     ctx_send, ctx_recv, sum_send, sum_recv, *slabs,
 ):
@@ -128,14 +129,17 @@
         first = coords[0, 2, 0, s] * per_block
         crows = jnp.concatenate([ctx_all[first + i] for i in range(per_block)], axis=0)
         crows = crows.reshape(BK // 16, 16, crows.shape[1])
-        parts = []
-        for b in range(rows):
-            brow = jnp.broadcast_to(brows[b:b + 1, :], (16, brows.shape[1])).astype(jnp.bfloat16)
-            parts.append((crows * brow[None]).reshape(BK, brows.shape[1]))
-        table = jnp.concatenate(parts, axis=0)
-        got = jnp.dot(
-            xbuf[s, :, h * depth:(h + 1) * depth], table, preferred_element_type=jnp.float32
-        )
+        got = None
+        for b in range(0, rows, PIECE):
+            parts = []
+            for i in range(b, b + PIECE):
+                brow = jnp.broadcast_to(brows[i:i + 1, :], (16, brows.shape[1]))
+                parts.append((crows * brow.astype(jnp.bfloat16)[None]).reshape(BK, brows.shape[1]))
+            piece = jnp.dot(
+                xbuf[s, :, h * depth + b * BK:h * depth + (b + PIECE) * BK],
+                jnp.concatenate(parts, axis=0), preferred_element_type=jnp.float32,
+            )
+            got = piece if got is None else got + piece
         if h == 0:
             term[s] = got
         else:
@@ -160,17 +164,17 @@
     used = counts[0, 0]
 
     def partial_sum(q):
-        total = jnp.zeros(out.shape, jnp.float32)
+        total = jnp.zeros(own.shape, jnp.float32)
         for s in range(slots):
             wanted = jnp.logical_and(
-                jnp.full(out.shape, coords[0, 0, 0, s]) == q, jnp.full(out.shape, used) > s
+                jnp.full(own.shape, coords[0, 0, 0, s]) == q, jnp.full(own.shape, used) > s
             )
             total += jnp.where(wanted, term[s], 0.0)
         return total
 
     def send_sum(j):
         return pltpu.make_async_remote_copy(
-            src_ref=outbox.at[j], dst_ref=inbox.at[j],
+            src_ref=outbox.at[j], dst_ref=inbox.at[j - 1],
             send_sem=sum_send.at[j], recv_sem=sum_recv.at[j],
             device_id=(me_r, column(j)), device_id_type=MESH,
         )
@@ -178,11 +182,12 @@
     for j in range(1, ncol):
         outbox[j] = partial_sum(column(j)).astype(outbox.dtype)
         send_sum(j).start()
-    total = partial_sum(me_c)
+    own[...] = partial_sum(me_c)
+    result = pltpu.make_async_copy(own, out, own_sem.at[0])
+    result.start()
     for j in range(1, ncol):
         send_sum(j).wait_recv()
-        total += inbox[j].astype(jnp.float32)
-    out[...] = total
+    result.wait()
 
     for j in range(1, ncol):
         for i in range(units):
@@ -202,9 +207,12 @@
     unit = min(BK, ctx_factor.shape[0])
     units = ctx_factor.shape[0] // unit
     dma = pltpu.SemaphoreType.DMA
-    return pl.pallas_call(
+    own, inbox = pl.pallas_call(
         functools.partial(kernel, nrow, ncol),
-        out_shape=jax.ShapeDtypeStruct((BQ, rank), jnp.float32),
+        out_shape=(
+            jax.ShapeDtypeStruct((BQ, rank), jnp.float32),
+            jax.ShapeDtypeStruct((ncol - 1, BQ, rank), SEND),
+        ),
         in_specs=[
             pl.BlockSpec(memory_space=pltpu.HBM),
             pl.BlockSpec(memory_space=pltpu.HBM),
@@ -212,7 +220,10 @@
             pl.BlockSpec(memory_space=pltpu.HBM),
             pl.BlockSpec(memory_space=pltpu.HBM),
         ],
-        out_specs=pl.BlockSpec(memory_space=pltpu.VMEM),
+        out_specs=(
+            pl.BlockSpec(memory_space=pltpu.HBM),
+            pl.BlockSpec(memory_space=pltpu.HBM),
+        ),
         scratch_shapes=[
             pltpu.SMEM((1, 3, 1, slots), jnp.int32),
             pltpu.SMEM((1, 1), jnp.int32),
@@ -220,7 +231,7 @@
             pltpu.VMEM((ctx_factor.shape[0] * ncol // unit, unit, rank), jnp.bfloat16),
             pltpu.VMEM((slots, BQ, rank), jnp.float32),
             pltpu.VMEM((ncol, BQ, rank), SEND),
-            pltpu.VMEM((ncol, BQ, rank), SEND),
+            pltpu.VMEM((BQ, rank), jnp.float32),
             dma((CHUNKS, slots)),
             dma((2 + CHUNKS,)),
             dma((CHUNKS, nz)),
@@ -242,6 +253,7 @@
             transcendentals=0,
         ),
     )(blocks, coords.transpose(0, 3, 1, 2), counts, doc_factor, ctx_factor)
+    return own + jnp.sum(inbox.astype(jnp.float32), axis=0)
 
 
 def solution(mesh):

time: 21.8 us -> 22.3 us (1.023)
  other arithmetic: 0 us -> 2.4 us
  local copies, waits for them, and re-layouts: 1.47 us -> 0 us
  Pallas kernels: 19.5 us -> 19 us
    add x0 -> x1, other arithmetic: none -> 1.48 us  [body(): return own + jnp.sum(inbox.astype(jnp.float32), axis=0)]
    unnamed x1 -> x0, local copies, waits for them, and re-layouts: 1.47 us -> none
    reduce_sum x0 -> x1, other arithmetic: none -> 0.91 us  [body(): return own + jnp.sum(inbox.astype(jnp.float32), axis=0)]
    pallas_call x1, Pallas kernels: 19.5 us -> 19 us  [body(): pl.pallas_call(functools.partial(kernel, nrow, ncol), out_shape=(jax.Shap...]
where the time goes in v4:
time: 22.3 us; the launch traced here: 22.1 us
  Pallas kernels  19 us (85%)
  other arithmetic  2.4 us (11%)
  between operations  0.66 us (3%)
    pallas_call x1, Pallas kernels, body(): pl.pallas_call(functools.partial(kernel, nrow, ncol), out_shape=(jax.Shap...  19 us
    add x1, other arithmetic, body(): return own + jnp.sum(inbox.astype(jnp.float32), axis=0)  1.48 us
    reduce_sum x1, other arithmetic, body(): return own + jnp.sum(inbox.astype(jnp.float32), axis=0)  0.91 us

profile of v4, /device:TPU:0, one launch (start us, length us, event | category | flops | bytes accessed | tf_op | source)
XLA Modules:
  0.0 22.1 jit_solution(17442149959188348874)
XLA Ops:
  0.7 19.0 %shard_map.55 = (f32[128,128]{1,0:T(8,128)}, bf16[3,128,128]{2,1,0:T(8,128)(2,1)}) custom-call(bf16[1,1,5,128,8192]{4,3,2,1,0:T(8,128)(2,1)} %blocks.1, s32[1,3,1,5]{3,2,1,0:T(1,128)} %bitcast.1, s32[1,1]{1,0:T(1,128)S(6)} %copy.6.counts_hbm, bf16[128,128]{1,0:T(8,128)(2,1)} %doc.1, bf16[128,128]{1,0:T(8,128)(2,1)} %ctx.1), custom_call_target="tpu_custom_call" | custom-call | flops 1342177280 | bytes 10485760 | tf_op jit(solution)/shard_map/pallas_call | solution.py:210
  19.7 0.9 %convert_reduce_fusion = f32[128,128]{1,0:T(8,128)S(1)} fusion(bf16[3,128,128]{2,1,0:T(8,128)(2,1)} %get-tuple-element.8), kind=kLoop, calls=%fused_computation | loop fusion | flops 81920 | bytes 163840 | tf_op jit(solution)/shard_map/reduce_sum | solution.py:256
  20.6 1.5 %add.3 = f32[128,128]{1,0:T(8,128)} add(f32[128,128]{1,0:T(8,128)} %get-tuple-element.7, f32[128,128]{1,0:T(8,128)S(1)} %convert_reduce_fusion) | non-fusion elementwise | flops 16384 | bytes 196608 | tf_op jit(solution)/shard_map/add | solution.py:256

commit v5 on v4

--- a/solution.py
+++ b/solution.py
@@ -68,9 +68,8 @@
     own_counts.start()
     for copy in own_docs + own_ctx:
         copy.start()
-    for h in range(CHUNKS):
-        for s in range(slots):
-            load(h, s).start()
+    for s in range(slots):
+        load(0, s).start()
 
     pl.semaphore_wait(barrier, len(peers))
 
@@ -115,6 +114,9 @@
             send_sibling(h, j).start()
 
     relay(0)
+    for h in range(1, CHUNKS):
+        for s in range(slots):
+            load(h, s).start()
     own_coords.wait()
     own_counts.wait()
     for copy in own_docs + own_ctx:
@@ -253,7 +255,9 @@
             transcendentals=0,
         ),
     )(blocks, coords.transpose(0, 3, 1, 2), counts, doc_factor, ctx_factor)
-    return own + jnp.sum(inbox.astype(jnp.float32), axis=0)
+    for j in range(ncol - 1):
+        own = own + inbox[j].astype(jnp.float32)
+    return own
 
 
 def solution(mesh):

time: 22.3 us -> 21.4 us (0.960)
  other arithmetic: 2.4 us -> 1.51 us
    reduce_sum x1 -> x0, other arithmetic: 0.91 us -> none  [body(): return own + jnp.sum(inbox.astype(jnp.float32), axis=0)]
where the time goes in v5:
time: 21.4 us; the launch traced here: 21.2 us
  Pallas kernels  19 us (89%)
  other arithmetic  1.51 us (7%)
  between operations  0.66 us (3%)
    pallas_call x1, Pallas kernels, body(): pl.pallas_call(functools.partial(kernel, nrow, ncol), out_shape=(jax.Shap...  19 us
    add x1, other arithmetic, body(): own = own + inbox[j].astype(jnp.float32)  1.51 us

profile of v5, /device:TPU:0, one launch (start us, length us, event | category | flops | bytes accessed | tf_op | source)
XLA Modules:
  0.0 21.2 jit_solution(9622293738253450357)
XLA Ops:
  0.7 19.0 %shard_map.55 = (f32[128,128]{1,0:T(8,128)}, bf16[3,128,128]{2,1,0:T(8,128)(2,1)}) custom-call(bf16[1,1,5,128,8192]{4,3,2,1,0:T(8,128)(2,1)} %blocks.1, s32[1,3,1,5]{3,2,1,0:T(1,128)} %bitcast.10, s32[1,1]{1,0:T(1,128)S(6)} %copy.6.counts_hbm, bf16[128,128]{1,0:T(8,128)(2,1)} %doc.1, bf16[128,128]{1,0:T(8,128)(2,1)} %ctx.1), custom_call_target="tpu_custom_call" | custom-call | flops 1342177280 | bytes 10485760 | tf_op jit(solution)/shard_map/pallas_call | solution.py:212
  19.7 1.5 %convert_add_fusion = f32[128,128]{1,0:T(8,128)} fusion(f32[128,128]{1,0:T(8,128)} %get-tuple-element.7, bf16[3,128,128]{2,1,0:T(8,128)(2,1)} %get-tuple-element.8), kind=kLoop, calls=%fused_computation | loop fusion | flops 98304 | bytes 229376 | tf_op jit(solution)/shard_map/add | solution.py:259

commit v6 on v5

--- a/solution.py
+++ b/solution.py
@@ -157,11 +157,11 @@
             return carry
 
         if h + 1 < CHUNKS:
-            lax.fori_loop(0, middle, step, 0)
+            lax.fori_loop(0, middle, step, 0, unroll=True)
             relay(h + 1)
-            lax.fori_loop(middle, slots, step, 0)
+            lax.fori_loop(middle, slots, step, 0, unroll=True)
         else:
-            lax.fori_loop(0, slots, step, 0)
+            lax.fori_loop(0, slots, step, 0, unroll=True)
 
     used = counts[0, 0]
 

time: 21.4 us -> 21.3 us (level)
  no operation moved by 1% of the time
where the time goes in v6:
time: 21.3 us; the launch traced here: 21.2 us
  Pallas kernels  19 us (89%)
  other arithmetic  1.51 us (7%)
  between operations  0.66 us (3%)
    pallas_call x1, Pallas kernels, body(): pl.pallas_call(functools.partial(kernel, nrow, ncol), out_shape=(jax.Shap...  19 us
    add x1, other arithmetic, body(): own = own + inbox[j].astype(jnp.float32)  1.51 us

profile of v6, /device:TPU:0, one launch (start us, length us, event | category | flops | bytes accessed | tf_op | source)
XLA Modules:
  0.0 21.2 jit_solution(13248872802450989405)
XLA Ops:
  0.7 19.0 %shard_map.55 = (f32[128,128]{1,0:T(8,128)}, bf16[3,128,128]{2,1,0:T(8,128)(2,1)}) custom-call(bf16[1,1,5,128,8192]{4,3,2,1,0:T(8,128)(2,1)} %blocks.1, s32[1,3,1,5]{3,2,1,0:T(1,128)} %bitcast.10, s32[1,1]{1,0:T(1,128)S(6)} %copy.6.counts_hbm, bf16[128,128]{1,0:T(8,128)(2,1)} %doc.1, bf16[128,128]{1,0:T(8,128)(2,1)} %ctx.1), custom_call_target="tpu_custom_call" | custom-call | flops 1342177280 | bytes 10485760 | tf_op jit(solution)/shard_map/pallas_call | solution.py:212
  19.7 1.5 %convert_add_fusion = f32[128,128]{1,0:T(8,128)} fusion(f32[128,128]{1,0:T(8,128)} %get-tuple-element.7, bf16[3,128,128]{2,1,0:T(8,128)(2,1)} %get-tuple-element.8), kind=kLoop, calls=%fused_computation | loop fusion | flops 98304 | bytes 229376 | tf_op jit(solution)/shard_map/add | solution.py:259
